TPU v7x, 128 devices: a whole 4x4x4 slice. The times are simulated.
128 devices in a mesh: dp: 8 (over x, core), fsdp: 16 (over y, z).
Axes of the slice: x: 4, y: 4, z: 4, core: 2. Of those that a mesh axis runs over, the one named last changes fastest.
Arguments:
- tokens: bfloat16 [16, 1024, 4096], P('fsdp', 'dp'), may hold values from -20 to 20
- segments: int32 [16, 1024], P('fsdp', 'dp'), may hold values from 0 to 3, never falling along the last dimension, each value on 1 to 512 neighbouring positions
- ln_gain: float32 [4096], replicated, may hold values from 0.1 to 1.9
- w_query: bfloat16 [4096, 4096], P('fsdp', 'dp'), may hold values from -2 to 2
- w_key: bfloat16 [4096, 4096], P('fsdp', 'dp'), may hold values from -0.5 to 0.5
- w_value: bfloat16 [4096, 4096], P('fsdp', 'dp'), may hold values from -0.09375 to 0.09375
- w_out: bfloat16 [4096, 4096], P('dp', 'fsdp'), may hold values from -0.09375 to 0.09375
Outputs:
- encoded: bfloat16 [16, 1024, 4096], P(None, ('dp', 'fsdp'))
Inputs may be any that keep to these rules, and one draw needn't show every extreme that they name: `segments`: caption numbers never fall along a group's rows; each group holds exactly 4 captions of 1 to 512 rows, and one caption of exactly 512 rows.
All inputs are finite; a program needn't handle non-finite values.
Results may differ from a plain program's by a relative error of at most 0.008.
Values may be sent and summed in bfloat16 or wider, within the bound.
No kernel may reach another device: no remote copies, remote signals or barrier semaphores. Data moves between devices by JAX's collectives and lax.ppermute only.
A program may use at most 128 MiB of HBM per device.

v0:
```python
import jax
import jax.numpy as jnp
from jax import lax
from jax.sharding import PartitionSpec as P

HEAD = 64


def body(tokens, segments, ln_gain, w_query, w_key, w_value, w_out):
    local_rows = tokens[0]
    seg_ids = segments[0]
    widened = local_rows.astype(jnp.float32)
    inv_rms = lax.rsqrt(jnp.mean(widened * widened, axis=-1, keepdims=True) + 1e-06)
    normed = (widened * inv_rms * ln_gain).astype(jnp.bfloat16)
    group_rows, group_seg = (
        lax.all_gather(normed, "dp", axis=0, tiled=True),
        lax.all_gather(seg_ids, "dp", axis=0, tiled=True),
    )
    row_count = group_rows.shape[0]
    inner_dev = w_query.shape[1]
    head_count = inner_dev // HEAD
    query = jnp.dot(
        group_rows,
        lax.all_gather(w_query, "fsdp", axis=0, tiled=True),
        preferred_element_type=jnp.float32,
    )
    keyed = jnp.dot(
        group_rows,
        lax.all_gather(w_key, "fsdp", axis=0, tiled=True),
        preferred_element_type=jnp.float32,
    )
    valued = jnp.dot(
        group_rows,
        lax.all_gather(w_value, "fsdp", axis=0, tiled=True),
        preferred_element_type=jnp.float32,
    )
    q_heads = query.astype(jnp.bfloat16).reshape(row_count, head_count, HEAD)
    k_heads = keyed.astype(jnp.bfloat16).reshape(row_count, head_count, HEAD)
    v_heads = valued.astype(jnp.bfloat16).reshape(row_count, head_count, HEAD)
    block_rows = min(512, row_count)
    block_total = row_count // block_rows
    q_blocks = q_heads.reshape(block_total, block_rows, head_count, HEAD)
    s_blocks = group_seg.reshape(block_total, block_rows)

    def attend_whole(packed_item):
        query_block, query_seg = packed_item
        scores = jnp.einsum(
            "qhd,khd->hqk", query_block, k_heads, preferred_element_type=jnp.float32
        )
        matched = query_seg[:, None] == group_seg[None, :]
        scores = jnp.where(matched[None], scores, -jnp.inf)
        row_peak = jnp.max(scores, axis=-1, keepdims=True)
        lifted = jnp.exp(scores - row_peak)
        row_total = jnp.sum(lifted, axis=-1, keepdims=True)
        soft_weights = (lifted / row_total).astype(jnp.bfloat16)
        return jnp.einsum(
            "hqk,khd->qhd", soft_weights, v_heads, preferred_element_type=jnp.float32
        ).astype(jnp.bfloat16)

    mixed = lax.map(attend_whole, (q_blocks, s_blocks))
    mixed = mixed.reshape(row_count, inner_dev)
    out_full = lax.all_gather(w_out, "fsdp", axis=1, tiled=True)
    summed = lax.psum_scatter(
        jnp.dot(mixed, out_full, preferred_element_type=jnp.float32).astype(jnp.bfloat16),
        "dp",
        scatter_dimension=0,
        tiled=True,
    ).astype(jnp.float32)
    encoded = (widened + summed).astype(jnp.bfloat16)
    return lax.all_to_all(encoded[None], "fsdp", split_axis=1, concat_axis=0, tiled=True)


def solution(mesh):
    placed = (
        P("fsdp", "dp", None),
        P("fsdp", "dp"),
        P(),
        P("fsdp", "dp"),
        P("fsdp", "dp"),
        P("fsdp", "dp"),
        P("dp", "fsdp"),
    )
    return jax.shard_map(
        body, mesh=mesh, in_specs=placed, out_specs=P(None, ("dp", "fsdp"), None), check_vma=False
    )
```

profile of v0, /device:TPU:0, one launch (start us, length us, event | category | flops | bytes accessed | tf_op | source)
XLA Modules:
  0.0 418.3 jit_solution(2871855484449245880)
XLA Ops:
  8.8 2.5 fusion.17
  13.4 10.6 %all-gather = s32[1,1024]{1,0:T(1,128)S(1)} all-gather(s32[1,128]{1,0:T(1,128)S(1)} %copy-done.1), channel_id=2, replica_groups=mesh['dp'=8,'fsdp'=16] {'dp'}, dimensions={1}, use_global_device_ids=true | all-gather | bytes 4608 | tf_op jit(solution)/shard_map/all_gather | solution.py:17
  25.2 38.4 %all-gather.9.cloned.1.call-done = bf16[4096,512]{1,0:T(8,128)(2,1)} async-done(((bf16[256,512]{1,0:T(8,128)(2,1)}), bf16[4096,512]{1,0:T(8,128)(2,1)}) %all-gather.9.cloned.1.call-update) | async-done | bytes 4194320 | tf_op jit(solution)/shard_map/all_gather | solution.py:24
  63.7 51.0 %all-gather.7.cloned.1.call-done = bf16[1024,4096]{1,0:T(8,128)(2,1)} async-done(((bf16[128,4096]{1,0:T(8,128)(2,1)}), bf16[1024,4096]{1,0:T(8,128)(2,1)}) %all-gather.7.cloned.1.call-update) | async-done | bytes 8388624 | tf_op jit(solution)/shard_map/all_gather | solution.py:16
  114.7 9.1 %convolution_convert_fusion.3 = bf16[1024,512]{1,0:T(8,128)(2,1)S(1)} fusion(bf16[1024,4096]{1,0:T(8,128)(2,1)} %all-gather.7.cloned.1.call-done, bf16[4096,512]{1,0:T(8,128)(2,1)} %all-gather.9.cloned.1.call-done), kind=kOutput, calls=%fused_computation.28 | convolution fusion | flops 4295491584 | bytes 13631488 | tf_op jit(solution)/shard_map/dot_general | solution.py:22
  123.7 1.6 reshape.65
  126.7 42.0 %all-gather.11.cloned.1.call-done = bf16[4096,512]{1,0:T(8,128)(2,1)} async-done(((bf16[256,512]{1,0:T(8,128)(2,1)}), bf16[4096,512]{1,0:T(8,128)(2,1)}) %all-gather.11.cloned.1.call-update) | async-done | bytes 4194320 | tf_op jit(solution)/shard_map/all_gather | solution.py:29
  168.7 9.1 %convolution_convert_fusion.2 = bf16[1024,512]{0,1:T(8,128)(2,1)S(1)} fusion(bf16[1024,4096]{1,0:T(8,128)(2,1)} %all-gather.7.cloned.1.call-done, bf16[4096,512]{1,0:T(8,128)(2,1)} %all-gather.11.cloned.1.call-done), kind=kOutput, calls=%fused_computation.27 | convolution fusion | flops 4295491584 | bytes 13631488 | tf_op jit(solution)/shard_map/dot_general | solution.py:27
  177.8 44.2 %all-gather.13.cloned.1.call-done = bf16[4096,512]{1,0:T(8,128)(2,1)} async-done(((bf16[256,512]{1,0:T(8,128)(2,1)}), bf16[4096,512]{1,0:T(8,128)(2,1)}) %all-gather.13.cloned.1.call-update) | async-done | bytes 4194320 | tf_op jit(solution)/shard_map/all_gather | solution.py:34
  222.0 10.1 %convolution_convert_fusion.1 = bf16[1024,512]{0,1:T(8,128)(2,1)} fusion(bf16[1024,4096]{1,0:T(8,128)(2,1)} %all-gather.7.cloned.1.call-done, bf16[4096,512]{1,0:T(8,128)(2,1)} %all-gather.13.cloned.1.call-done), kind=kOutput, calls=%fused_computation.26 | convolution fusion | flops 4295491584 | bytes 13631488 | tf_op jit(solution)/shard_map/dot_general | solution.py:32
  232.0 76.3 %while.10 = (s32[]{:T(128)}, bf16[2,512,8,64]{1,3,2,0:T(8,128)(2,1)}, s32[2,512]{1,0:T(2,128)S(1)}, s32[1024]{0:T(1024)S(1)}, bf16[2,512,8,64]{1,3,2,0:T(8,128)(...) while((s32[]{:T(128)}, bf16[2,512,8,64]{1,3,2,0:T(8,128)(2,1)}, ...), condition=%wide.region_4.5_spmd, body=%wide.region_1.4_spmd.sunk | while | flops 1099695104 | bytes 71346776 | solution.py:60
  232.2 8.1 %fusion.40 = f32[8,512,1024]{2,1,0:T(8,128)} fusion(bf16[1024,8,64]{0,2,1:T(8,128)(2,1)S(1)} %get-tuple-element.155, bf16[2,512,8,64]{1,3,2,0:T(8,128)(2,1)S(1)} %get-tuple-element.154, s32[]{:T(128)} %get-tuple-element.142), kind=kOutput, calls=%fused_computation.12.clone.1 | convolution fusion | flops 536870912 | bytes 18350084 | tf_op jit(solution)/shard_map/while/body/eval_jaxpr/qhd,khd->hqk/dot_general | solution.py:47
  240.7 19.9 %fusion.41 = (f32[8,512]{1,0:T(8,128)S(1)}, f32[8,512,1024]{2,1,0:T(8,128)}) fusion(f32[8,512,1024]{2,1,0:T(8,128)} %fusion.40, pred[512,1024]{1,0:T(8,128)(4,1)S(1)} %broadcast_compare_fusion.2), kind=kOutput, calls=%fused_computation.32.clone.1 | output fusion | flops 16778240 | bytes 34095104 | tf_op jit(solution)/shard_map/while/body/eval_jaxpr/sub | solution.py:53
  260.6 9.6 %fusion.42 = bf16[2,512,8,64]{1,3,2,0:T(8,128)(2,1)} fusion(bf16[2,512,8,64]{1,3,2,0:T(8,128)(2,1)} %get-tuple-element.143, s32[]{:T(128)} %get-tuple-element.142, bf16[1024,8,64]{0,2,1:T(8,128)(2,1)} %get-tuple-element.156, f32[8,512,1024]{2,1,0:T(8,128)} %get-tuple-element.132, f32[8,512]{1,0:T(8,128)S(1)} %get-tuple-element.133), kind=kOutput, calls=%fused_computation.10.clone.1 | convolution fusion | flops 545521664 | bytes 18366976 | tf_op jit(solution)/shard_map/while/body/eval_jaxpr/hqk,khd->qhd/dot_general | solution.py:56
  270.2 8.2 %fusion.40 = f32[8,512,1024]{2,1,0:T(8,128)} fusion(bf16[1024,8,64]{0,2,1:T(8,128)(2,1)S(1)} %get-tuple-element.155, bf16[2,512,8,64]{1,3,2,0:T(8,128)(2,1)S(1)} %get-tuple-element.154, s32[]{:T(128)} %get-tuple-element.142), kind=kOutput, calls=%fused_computation.12.clone.1 | convolution fusion | flops 536870912 | bytes 18350084 | tf_op jit(solution)/shard_map/while/body/eval_jaxpr/qhd,khd->hqk/dot_general | solution.py:47
  278.9 19.9 %fusion.41 = (f32[8,512]{1,0:T(8,128)S(1)}, f32[8,512,1024]{2,1,0:T(8,128)}) fusion(f32[8,512,1024]{2,1,0:T(8,128)} %fusion.40, pred[512,1024]{1,0:T(8,128)(4,1)S(1)} %broadcast_compare_fusion.2), kind=kOutput, calls=%fused_computation.32.clone.1 | output fusion | flops 16778240 | bytes 34095104 | tf_op jit(solution)/shard_map/while/body/eval_jaxpr/sub | solution.py:53
  298.8 9.5 %fusion.42 = bf16[2,512,8,64]{1,3,2,0:T(8,128)(2,1)} fusion(bf16[2,512,8,64]{1,3,2,0:T(8,128)(2,1)} %get-tuple-element.143, s32[]{:T(128)} %get-tuple-element.142, bf16[1024,8,64]{0,2,1:T(8,128)(2,1)} %get-tuple-element.156, f32[8,512,1024]{2,1,0:T(8,128)} %get-tuple-element.132, f32[8,512]{1,0:T(8,128)S(1)} %get-tuple-element.133), kind=kOutput, calls=%fused_computation.10.clone.1 | convolution fusion | flops 545521664 | bytes 18366976 | tf_op jit(solution)/shard_map/while/body/eval_jaxpr/hqk,khd->qhd/dot_general | solution.py:56
  308.3 2.3 copy.18
  310.9 9.1 %convolution_convert_fusion = bf16[1024,4096]{1,0:T(8,128)(2,1)} fusion(bf16[1024,512]{0,1:T(8,128)(2,1)S(1)} %bitcast.56, bf16[512,4096]{1,0:T(8,128)(2,1)} %all-gather.15.cloned.1.call-done), kind=kOutput, calls=%fused_computation.18 | convolution fusion | flops 4299161600 | bytes 13631488 | tf_op jit(solution)/shard_map/dot_general | solution.py:64
  320.1 52.2 %reduce-scatter.2.cloned.1.call-done = bf16[128,4096]{1,0:T(8,128)(2,1)} async-done(((bf16[1024,4096]{1,0:T(8,128)(2,1)}), bf16[128,4096]{1,0:T(8,128)(2,1)}) %reduce-scatter.2.cloned.1.call-update) | async-done | bytes 1048592 | tf_op jit(solution)/shard_map/reduce_scatter | solution.py:63
  373.7 2.4 copy.27
  376.6 7.0 %reduce.4 = bf16[128,4096]{1,0:T(8,128)(2,1)S(1)} reduce(bf16[128,1,4096]{2,1,0:T(2,128)(2,1)S(1)} %bitcast.54, bf16[]{:T(256)} %broadcast.37), dimensions={1}, to_apply=%bitcast.41.reduce_sub_computation | reduce | bytes 2097154
  384.8 23.3 %all_to_all.12 = bf16[16,2,16384]{2,1,0:T(2,128)(2,1)S(1)} all-to-all(bf16[16,2,16384]{2,1,0:T(2,128)(2,1)S(1)} %reshape.75), channel_id=1, replica_groups=mesh['dp'=8,'fsdp'=16] {'fsdp'}, dimensions={0} | all-to-all | bytes 2097152 | tf_op jit(solution)/shard_map/all_to_all | solution.py:70
  409.2 2.1 copy.26
  (33 shorter events, 12.1 us)
Async XLA Ops:
  6.5 6.8 %copy-start.1 = (s32[1,128]{1,0:T(1,128)S(1)}, s32[1,128]{1,0:T(1,128)}, u32[]{:S(2)}) copy-start(s32[1,128]{1,0:T(1,128)} %param.10) | copy-start | bytes 1540
  6.5 57.1 %all-gather.9.cloned.1.call-start = ((), (), s32[]{:S(2)}) async-start(), calls=%async_computation.3 | async-start | bytes 4456448 | tf_op jit(solution)/shard_map/all_gather | solution.py:24
  7.3 107.4 %all-gather.7.cloned.1.call-start = ((), (), s32[]{:S(2)}) async-start(), calls=%async_computation.2 | async-start | bytes 9437184 | tf_op jit(solution)/shard_map/all_gather | solution.py:16
  11.4 157.3 %all-gather.11.cloned.1.call-start = ((), (), s32[]{:S(2)}) async-start(), calls=%async_computation.4 | async-start | bytes 4456448 | tf_op jit(solution)/shard_map/all_gather | solution.py:29
  12.1 209.8 %all-gather.13.cloned.1.call-start = ((), (), s32[]{:S(2)}) async-start(), calls=%async_computation.5 | async-start | bytes 4456448 | tf_op jit(solution)/shard_map/all_gather | solution.py:34
  12.7 298.2 %all-gather.15.cloned.1.call-start = ((), (), s32[]{:S(2)}) async-start(), calls=%async_computation.6 | async-start | bytes 4456448 | tf_op jit(solution)/shard_map/all_gather | solution.py:62
  13.3 358.9 %reduce-scatter.2.cloned.1.call-start = ((), (), s32[]{:S(2)}) async-start(), calls=%async_computation.7 | async-start | bytes 9437184 | tf_op jit(solution)/shard_map/reduce_scatter | solution.py:63
  320.0 52.2 %copy-start = (bf16[1,128,4096]{2,1,0:T(8,128)(2,1)S(1)}, bf16[1,128,4096]{2,1,0:T(8,128)(2,1)}, u32[]{:S(2)}) copy-start(bf16[1,128,4096]{2,1,0:T(8,128)(2,1)} %param.9) | copy-start | bytes 3145732
Sparse Core Ops, SparseCore 0:
  9.5 54.1 all-gather.8
  65.4 49.2 all-gather.6
  116.8 51.8 all-gather.10
  170.7 51.2 all-gather.12
  223.9 57.2 all-gather.14
  320.2 52.0 reduce-scatter.1
where the time goes:
time: 422 us; the launch traced here: 418 us
  waiting for transfers between devices  230 us (55%)
  matrix products  72.8 us (17%)
  other arithmetic  53.8 us (13%)
  blocking collectives  33.9 us (8%)
  between operations  13.8 us (3%)
  local copies, waits for them, and re-layouts  13.3 us (3%)
    reduce_scatter x1, waiting for transfers between devices, body(): lax.psum_scatter(jnp.dot(mixed, out_full, preferred_element_type=jnp.floa...  52.2 us
    all_gather x1, waiting for transfers between devices, body(): lax.all_gather(normed, 'dp', axis=0, tiled=True)  51 us
    all_gather x1, waiting for transfers between devices, body(): lax.all_gather(w_value, 'fsdp', axis=0, tiled=True)  44.2 us
    all_gather x1, waiting for transfers between devices, body(): lax.all_gather(w_key, 'fsdp', axis=0, tiled=True)  42 us
    sub x2, other arithmetic, attend_whole(): lifted = jnp.exp(scores - row_peak)  39.8 us
    all_gather x1, waiting for transfers between devices, body(): lax.all_gather(w_query, 'fsdp', axis=0, tiled=True)  38.4 us
    all_to_all x1, blocking collectives, body(): lax.all_to_all(encoded[None], 'fsdp', split_axis=1, concat_axis=0, tiled=...  23.3 us
    dot_general x2, matrix products, attend_whole(): jnp.einsum('hqk,khd->qhd', soft_weights, v_heads, preferred_element_type=...  19.2 us
  transfers between devices with their start and end apart: 6, of which 5 were waited for; matrix products, arithmetic and copies ran while one was open for 28% of the time, Pallas kernels for 0%

commit v1 on v0

--- a/solution.py
+++ b/solution.py
@@ -67,7 +67,12 @@
         tiled=True,
     ).astype(jnp.float32)
     encoded = (widened + summed).astype(jnp.bfloat16)
-    return lax.all_to_all(encoded[None], "fsdp", split_axis=1, concat_axis=0, tiled=True)
+    return jnp.concatenate(
+        lax.all_to_all(
+            jnp.stack(jnp.split(encoded[None], lax.axis_size("fsdp"), axis=1)), "fsdp", 0, 0
+        ),
+        axis=0,
+    )
 
 
 def solution(mesh):

time: 422 us -> 405 us (0.960)
  other arithmetic: 53.8 us -> 46.8 us
  local copies, waits for them, and re-layouts: 13.3 us -> 6.95 us
    unnamed x1 -> x0, other arithmetic: 7.02 us -> none
where the time goes in v1:
time: 405 us
  waiting for transfers between devices  231 us (57%)
  matrix products  72.7 us (18%)
  other arithmetic  46.8 us (12%)
  blocking collectives  33.9 us (8%)
  between operations  13.7 us (3%)
  local copies, waits for them, and re-layouts  6.95 us (2%)
    reduce_scatter x1, waiting for transfers between devices, body(): lax.psum_scatter(jnp.dot(mixed, out_full, preferred_element_type=jnp.floa...  52.2 us
    all_gather x1, waiting for transfers between devices, body(): lax.all_gather(normed, 'dp', axis=0, tiled=True)  51 us
    all_gather x1, waiting for transfers between devices, body(): lax.all_gather(w_value, 'fsdp', axis=0, tiled=True)  44.2 us
    all_gather x1, waiting for transfers between devices, body(): lax.all_gather(w_key, 'fsdp', axis=0, tiled=True)  42.2 us
    sub x2, other arithmetic, attend_whole(): lifted = jnp.exp(scores - row_peak)  39.9 us
    all_gather x1, waiting for transfers between devices, body(): lax.all_gather(w_query, 'fsdp', axis=0, tiled=True)  38.5 us
    all_to_all x1, blocking collectives, body(): lax.all_to_all(jnp.stack(jnp.split(encoded[None], lax.axis_size('fsdp'),...  23.3 us
    dot_general x2, matrix products, attend_whole(): jnp.einsum('hqk,khd->qhd', soft_weights, v_heads, preferred_element_type=...  19.1 us
  transfers between devices with their start and end apart: 6, of which 5 were waited for; matrix products, arithmetic and copies ran while one was open for 28% of the time, Pallas kernels for 0%

profile of v1, /device:TPU:0, one launch (start us, length us, event | category | flops | bytes accessed | tf_op | source)
XLA Modules:
  0.0 404.8 jit_solution(17164341447727309978)
XLA Ops:
  7.3 1.5 fusion.15
  8.8 2.5 fusion.17
  13.4 10.6 %all-gather = s32[1,1024]{1,0:T(1,128)S(1)} all-gather(s32[1,128]{1,0:T(1,128)S(1)} %copy-done.1), channel_id=2, replica_groups=mesh['dp'=8,'fsdp'=16] {'dp'}, dimensions={1}, use_global_device_ids=true | all-gather | bytes 4608 | tf_op jit(solution)/shard_map/all_gather | solution.py:17
  25.2 38.5 %all-gather.9.cloned.1.call-done = bf16[4096,512]{1,0:T(8,128)(2,1)} async-done(((bf16[256,512]{1,0:T(8,128)(2,1)}), bf16[4096,512]{1,0:T(8,128)(2,1)}) %all-gather.9.cloned.1.call-update) | async-done | bytes 4194320 | tf_op jit(solution)/shard_map/all_gather | solution.py:24
  63.7 51.0 %all-gather.7.cloned.1.call-done = bf16[1024,4096]{1,0:T(8,128)(2,1)} async-done(((bf16[128,4096]{1,0:T(8,128)(2,1)}), bf16[1024,4096]{1,0:T(8,128)(2,1)}) %all-gather.7.cloned.1.call-update) | async-done | bytes 8388624 | tf_op jit(solution)/shard_map/all_gather | solution.py:16
  114.7 9.1 %convolution_convert_fusion.3 = bf16[1024,512]{1,0:T(8,128)(2,1)S(1)} fusion(bf16[1024,4096]{1,0:T(8,128)(2,1)} %all-gather.7.cloned.1.call-done, bf16[4096,512]{1,0:T(8,128)(2,1)} %all-gather.9.cloned.1.call-done), kind=kOutput, calls=%fused_computation.28 | convolution fusion | flops 4295491584 | bytes 13631488 | tf_op jit(solution)/shard_map/dot_general | solution.py:22
  123.7 1.3 reshape.66
  125.0 1.4 copy.10
  126.5 42.2 %all-gather.11.cloned.1.call-done = bf16[4096,512]{1,0:T(8,128)(2,1)} async-done(((bf16[256,512]{1,0:T(8,128)(2,1)}), bf16[4096,512]{1,0:T(8,128)(2,1)}) %all-gather.11.cloned.1.call-update) | async-done | bytes 4194320 | tf_op jit(solution)/shard_map/all_gather | solution.py:29
  168.7 9.1 %convolution_convert_fusion.2 = bf16[1024,512]{0,1:T(8,128)(2,1)S(1)} fusion(bf16[1024,4096]{1,0:T(8,128)(2,1)} %all-gather.7.cloned.1.call-done, bf16[4096,512]{1,0:T(8,128)(2,1)} %all-gather.11.cloned.1.call-done), kind=kOutput, calls=%fused_computation.27 | convolution fusion | flops 4295491584 | bytes 13631488 | tf_op jit(solution)/shard_map/dot_general | solution.py:27
  177.8 44.2 %all-gather.13.cloned.1.call-done = bf16[4096,512]{1,0:T(8,128)(2,1)} async-done(((bf16[256,512]{1,0:T(8,128)(2,1)}), bf16[4096,512]{1,0:T(8,128)(2,1)}) %all-gather.13.cloned.1.call-update) | async-done | bytes 4194320 | tf_op jit(solution)/shard_map/all_gather | solution.py:34
  222.0 10.1 %convolution_convert_fusion.1 = bf16[1024,512]{0,1:T(8,128)(2,1)} fusion(bf16[1024,4096]{1,0:T(8,128)(2,1)} %all-gather.7.cloned.1.call-done, bf16[4096,512]{1,0:T(8,128)(2,1)} %all-gather.13.cloned.1.call-done), kind=kOutput, calls=%fused_computation.26 | convolution fusion | flops 4295491584 | bytes 13631488 | tf_op jit(solution)/shard_map/dot_general | solution.py:32
  232.1 76.1 %while.10 = (s32[]{:T(128)}, bf16[2,512,8,64]{1,3,2,0:T(8,128)(2,1)}, s32[2,512]{1,0:T(2,128)S(1)}, s32[1024]{0:T(1024)S(1)}, bf16[2,512,8,64]{1,3,2,0:T(8,128)(...) while((s32[]{:T(128)}, bf16[2,512,8,64]{1,3,2,0:T(8,128)(2,1)}, ...), condition=%wide.region_4.5_spmd, body=%wide.region_1.4_spmd.sunk | while | flops 1099695104 | bytes 71346776 | solution.py:60
  232.1 8.1 %fusion.56 = f32[8,512,1024]{2,1,0:T(8,128)} fusion(bf16[1024,8,64]{0,2,1:T(8,128)(2,1)S(1)} %get-tuple-element.141, bf16[2,512,8,64]{1,3,2,0:T(8,128)(2,1)S(1)} %get-tuple-element.140, s32[]{:T(128)} %get-tuple-element.128), kind=kOutput, calls=%fused_computation.12.clone.1 | convolution fusion | flops 536870912 | bytes 18350084 | tf_op jit(solution)/shard_map/while/body/eval_jaxpr/qhd,khd->hqk/dot_general | solution.py:47
  240.5 19.9 %fusion.57 = (f32[8,512]{1,0:T(8,128)S(1)}, f32[8,512,1024]{2,1,0:T(8,128)}) fusion(f32[8,512,1024]{2,1,0:T(8,128)} %fusion.56, pred[512,1024]{1,0:T(8,128)(4,1)S(1)} %broadcast_compare_fusion.2), kind=kOutput, calls=%fused_computation.63.clone.1 | output fusion | flops 16778240 | bytes 34095104 | tf_op jit(solution)/shard_map/while/body/eval_jaxpr/sub | solution.py:53
  260.5 9.6 %fusion.58 = bf16[2,512,8,64]{1,3,2,0:T(8,128)(2,1)} fusion(bf16[2,512,8,64]{1,3,2,0:T(8,128)(2,1)} %get-tuple-element.129, s32[]{:T(128)} %get-tuple-element.128, bf16[1024,8,64]{0,2,1:T(8,128)(2,1)} %get-tuple-element.142, f32[8,512,1024]{2,1,0:T(8,128)} %get-tuple-element.118, f32[8,512]{1,0:T(8,128)S(1)} %get-tuple-element.119), kind=kOutput, calls=%fused_computation.10.clone.1 | convolution fusion | flops 545521664 | bytes 18366976 | tf_op jit(solution)/shard_map/while/body/eval_jaxpr/hqk,khd->qhd/dot_general | solution.py:56
  270.1 8.3 %fusion.56 = f32[8,512,1024]{2,1,0:T(8,128)} fusion(bf16[1024,8,64]{0,2,1:T(8,128)(2,1)S(1)} %get-tuple-element.141, bf16[2,512,8,64]{1,3,2,0:T(8,128)(2,1)S(1)} %get-tuple-element.140, s32[]{:T(128)} %get-tuple-element.128), kind=kOutput, calls=%fused_computation.12.clone.1 | convolution fusion | flops 536870912 | bytes 18350084 | tf_op jit(solution)/shard_map/while/body/eval_jaxpr/qhd,khd->hqk/dot_general | solution.py:47
  278.7 19.9 %fusion.57 = (f32[8,512]{1,0:T(8,128)S(1)}, f32[8,512,1024]{2,1,0:T(8,128)}) fusion(f32[8,512,1024]{2,1,0:T(8,128)} %fusion.56, pred[512,1024]{1,0:T(8,128)(4,1)S(1)} %broadcast_compare_fusion.2), kind=kOutput, calls=%fused_computation.63.clone.1 | output fusion | flops 16778240 | bytes 34095104 | tf_op jit(solution)/shard_map/while/body/eval_jaxpr/sub | solution.py:53
  298.7 9.5 %fusion.58 = bf16[2,512,8,64]{1,3,2,0:T(8,128)(2,1)} fusion(bf16[2,512,8,64]{1,3,2,0:T(8,128)(2,1)} %get-tuple-element.129, s32[]{:T(128)} %get-tuple-element.128, bf16[1024,8,64]{0,2,1:T(8,128)(2,1)} %get-tuple-element.142, f32[8,512,1024]{2,1,0:T(8,128)} %get-tuple-element.118, f32[8,512]{1,0:T(8,128)S(1)} %get-tuple-element.119), kind=kOutput, calls=%fused_computation.10.clone.1 | convolution fusion | flops 545521664 | bytes 18366976 | tf_op jit(solution)/shard_map/while/body/eval_jaxpr/hqk,khd->qhd/dot_general | solution.py:56
  308.2 2.3 copy.11
  310.8 9.0 %convolution_convert_fusion = bf16[1024,4096]{1,0:T(8,128)(2,1)} fusion(bf16[1024,512]{0,1:T(8,128)(2,1)S(1)} %bitcast.113, bf16[512,4096]{1,0:T(8,128)(2,1)} %all-gather.15.cloned.1.call-done), kind=kOutput, calls=%fused_computation.18 | convolution fusion | flops 4299161600 | bytes 13631488 | tf_op jit(solution)/shard_map/dot_general | solution.py:64
  319.8 52.2 %reduce-scatter.2.cloned.1.call-done = bf16[128,4096]{1,0:T(8,128)(2,1)} async-done(((bf16[1024,4096]{1,0:T(8,128)(2,1)}), bf16[128,4096]{1,0:T(8,128)(2,1)}) %reduce-scatter.2.cloned.1.call-update) | async-done | bytes 1048592 | tf_op jit(solution)/shard_map/reduce_scatter | solution.py:63
  372.0 1.5 fusion.19
  373.7 23.3 %all_to_all.5 = bf16[16,1,8,4096]{3,2,1,0:T(8,128)(2,1)S(1)} all-to-all(bf16[16,1,8,4096]{3,2,1,0:T(8,128)(2,1)S(1)} %fusion.20), channel_id=1, replica_groups=mesh['dp'=8,'fsdp'=16] {'fsdp'}, dimensions={0} | all-to-all | bytes 2097152 | tf_op jit(solution)/shard_map/all_to_all | solution.py:71
  (44 shorter events, 6.0 us)
Async XLA Ops:
  6.5 6.8 %copy-start.1 = (s32[1,128]{1,0:T(1,128)S(1)}, s32[1,128]{1,0:T(1,128)}, u32[]{:S(2)}) copy-start(s32[1,128]{1,0:T(1,128)} %param.10) | copy-start | bytes 1540
  6.5 57.1 %all-gather.9.cloned.1.call-start = ((), (), s32[]{:S(2)}) async-start(), calls=%async_computation.3 | async-start | bytes 4456448 | tf_op jit(solution)/shard_map/all_gather | solution.py:24
  7.3 107.4 %all-gather.7.cloned.1.call-start = ((), (), s32[]{:S(2)}) async-start(), calls=%async_computation.2 | async-start | bytes 9437184 | tf_op jit(solution)/shard_map/all_gather | solution.py:16
  11.4 157.3 %all-gather.11.cloned.1.call-start = ((), (), s32[]{:S(2)}) async-start(), calls=%async_computation.4 | async-start | bytes 4456448 | tf_op jit(solution)/shard_map/all_gather | solution.py:29
  12.1 209.9 %all-gather.13.cloned.1.call-start = ((), (), s32[]{:S(2)}) async-start(), calls=%async_computation.5 | async-start | bytes 4456448 | tf_op jit(solution)/shard_map/all_gather | solution.py:34
  12.7 298.1 %all-gather.15.cloned.1.call-start = ((), (), s32[]{:S(2)}) async-start(), calls=%async_computation.6 | async-start | bytes 4456448 | tf_op jit(solution)/shard_map/all_gather | solution.py:62
  13.3 358.7 %reduce-scatter.2.cloned.1.call-start = ((), (), s32[]{:S(2)}) async-start(), calls=%async_computation.7 | async-start | bytes 9437184 | tf_op jit(solution)/shard_map/reduce_scatter | solution.py:63
  319.7 52.2 %copy-start = (bf16[1,128,4096]{2,1,0:T(8,128)(2,1)S(1)}, bf16[1,128,4096]{2,1,0:T(8,128)(2,1)}, u32[]{:S(2)}) copy-start(bf16[1,128,4096]{2,1,0:T(8,128)(2,1)} %param.9) | copy-start | bytes 3145732
Sparse Core Ops, SparseCore 0:
  9.5 54.1 all-gather.8
  65.4 49.2 all-gather.6
  116.8 51.8 all-gather.10
  170.7 51.2 all-gather.12
  223.9 57.2 all-gather.14
  319.9 52.0 reduce-scatter.1
